TPU v7x, 32 devices: a whole 2x2x4 slice. The times are simulated.
32 devices in a mesh: gx: 4 (over z), gy: 4 (over x, core), ha: 2 (over y).
Axes of the slice: x: 2, y: 2, z: 4, core: 2. Of those that a mesh axis runs over, the one named last changes fastest.
Arguments:
- offsets: float32 [3, 8, 8, 4, 128], P(None, 'gx', 'gy', 'ha'), may hold values from 0 to 1
- forces: float32 [3, 8, 8, 4, 128], P(None, 'gx', 'gy', 'ha'), may hold values from -6 to 6
- counts: int32 [8, 8, 4], P('gx', 'gy', 'ha'), may hold values from 16 to 128, as said below
Outputs:
- velocity: float32 [3, 8, 8, 4, 128], P(None, 'gx', 'gy', 'ha')
Inputs may be any that keep to these rules, and one draw needn't show every extreme that they name: `counts`: A bin is heavy when its count exceeds 64. The 16 bins that two devices differing only in their ha index hold together include at most 8 heavy bins; in every draw some such pair holds exactly 8, all on one device; some bin holds exactly 128.
All inputs are finite; a program needn't handle non-finite values.
Results may differ from a plain program's by a relative error of at most 0.0003.
Values sent between devices are 32-bit elements; how exact they have to be, the bound alone decides.
No kernel may reach another device: no remote copies, remote signals or barrier semaphores. Data moves between devices by JAX's collectives and lax.ppermute only.
A program may use at most 64 MiB of HBM per device.

v0:
```python
import functools
import math

import jax
import jax.numpy as jnp
from jax import lax
from jax.experimental import pallas as pl
from jax.experimental.pallas import tpu as pltpu
from jax.sharding import PartitionSpec as P

SPLIT_XI = 2.0
SOFT_SQ = 0.01
GAUSS_COEF = 2.0 * SPLIT_XI / math.sqrt(math.pi)
STOKES_NORM = 1.0 / (8.0 * math.pi)

SOFT_U = SPLIT_XI * SPLIT_XI * SOFT_SQ
LOG2_E = math.log2(math.e)
LOG2_G = math.log2(GAUSS_COEF)
SELF_C = math.erfc(math.sqrt(SOFT_U)) / math.sqrt(SOFT_SQ) + GAUSS_COEF * (
    2.0 * SOFT_U - 3.0
) * math.exp(-SOFT_U)

LANES = 128
ROWS = 8
CHUNK = 64
WIDE = 2
BLOCK = WIDE * LANES
GROUP = 16
COUNT_ROW = 3
FORCE_ROW = 4


def rows_and_lanes(shape=(ROWS, LANES)):
    return lax.broadcasted_iota(jnp.int32, shape, 0), lax.broadcasted_iota(jnp.int32, shape, 1)


def pack_kernel(cells, count_ref, offset_ref, force_ref, out_ref):
    slot = lax.broadcasted_iota(jnp.int32, (1, LANES), 1)
    for ix in range(cells[0]):
        for iy in range(cells[1]):
            for iz in range(cells[2]):
                count = count_ref[ix, iy, iz]
                filled = jnp.full((1, LANES), count, jnp.int32).astype(jnp.float32)
                for i in range(3):
                    position = offset_ref[i, ix, iy, iz : iz + 1, :]
                    out_ref[ix, iy, iz, i : i + 1, :] = position * SPLIT_XI - 0.5 * SPLIT_XI
                    force = force_ref[i, ix, iy, iz : iz + 1, :]
                    at = FORCE_ROW + i
                    out_ref[ix, iy, iz, at : at + 1, :] = jnp.where(slot < count, force, 0.0)
                out_ref[ix, iy, iz, 3:4, :] = filled
                out_ref[ix, iy, iz, 7:8, :] = filled


def compact(listed, base, sources):
    _, lane = rows_and_lanes()
    current = jnp.zeros((ROWS, LANES), jnp.float32)
    filled = jnp.int32(0)
    for tile, count in sources:
        tile_id = base + lax.shift_right_logical(filled, 7)
        at = lax.bitwise_and(filled, LANES - 1)
        moved = pltpu.roll(tile, at, 1)
        behind = lane >= at
        current = jnp.where(behind, moved, current)
        spill = jnp.where(behind, 0.0, moved)
        listed[tile_id] = current
        listed[tile_id + 1] = spill
        filled = filled + count
        current = jnp.where(at + count >= LANES, spill, current)
    last = base + lax.shift_right_logical(filled, 7)
    for more in range(1, WIDE):
        listed[last + more] = jnp.zeros((ROWS, LANES), jnp.float32)
    return filled


def spread_targets(spread, first, tile):
    columns = jnp.transpose(jnp.concatenate([tile] * (LANES // ROWS), axis=0))
    for i in range(3):
        spread[i, pl.ds(first, LANES), :] = jnp.broadcast_to(columns[:, i : i + 1], (LANES, LANES))


def pair_terms(target, source, force):
    delta = [t - s for t, s in zip(target, source)]
    u = (delta[0] * delta[0] + SOFT_U) + delta[1] * delta[1] + delta[2] * delta[2]
    inv = lax.rsqrt(u)
    tail = (1.0 - lax.erf(u * inv)) * inv
    gauss = jnp.exp2(LOG2_G - u * LOG2_E)
    rest = gauss * (u - 1.5)
    coef_c = tail + rest
    coef_d = ((tail - rest) - gauss) * (inv * inv)
    along = coef_d * (delta[0] * force[0] + delta[1] * force[1] + delta[2] * force[2])
    return [coef_c * f + along * d for f, d in zip(force, delta)]


def all_pairs(n_groups, chunks_of, blocks_of, max_chunks, max_blocks, refs):
    listed, spread, acc, summed = refs

    def process(group, chunk, block):
        sources = []
        for b in range(WIDE):
            tile_id = (group * max_blocks + block) * WIDE + b
            rows = [listed[tile_id, i : i + 1, :] for i in (0, 1, 2, 4, 5, 6)]
            sources.append((rows[:3], rows[3:]))
        first = (group * max_chunks + chunk) * CHUNK
        for r in range(0, CHUNK, GROUP):
            at = pl.ds(pl.multiple_of(first + r, GROUP), GROUP)
            target = [spread[i, at, :] for i in range(3)]
            sums = None
            for source, force in sources:
                terms = pair_terms(target, source, force)
                sums = terms if sums is None else [s + t for s, t in zip(sums, terms)]
            for i in range(3):
                acc[i, r : r + GROUP, :] = acc[i, r : r + GROUP, :] + sums[i]

    def reduce(group, chunk):
        _, lane = rows_and_lanes((CHUNK, LANES))
        merged = jnp.zeros((CHUNK, LANES), jnp.float32)
        for i in range(3):
            merged = jnp.where(lane == i, jnp.sum(acc[i], axis=1, keepdims=True), merged)
            acc[i] = jnp.zeros((CHUNK, LANES), jnp.float32)
        at = pl.multiple_of((group * max_chunks + chunk) * CHUNK, CHUNK)
        summed[pl.ds(at, CHUNK), :] = merged

    total = jnp.int32(0)
    for group in range(n_groups):
        total = total + chunks_of[group] * blocks_of[group]
    acc[...] = jnp.zeros_like(acc)

    def one_item(item, state):
        group, chunk, block = state
        end_block = block + 1 == blocks_of[group]
        next_block = jnp.where(end_block, 0, block + 1)
        next_chunk = jnp.where(end_block, chunk + 1, chunk)
        end_chunk = next_chunk == chunks_of[group]
        next_chunk = jnp.where(end_chunk, 0, next_chunk)
        next_group = jnp.where(end_chunk, jnp.minimum(group + 1, n_groups - 1), group)
        process(group, chunk, block)

        @pl.when(end_block)
        def _():
            reduce(group, chunk)

        return next_group, next_chunk, next_block

    zero = jnp.int32(0)
    lax.fori_loop(0, total, one_item, (zero, zero, zero))


def inner_kernel(cells, count_ref, own_ref, out_ref, chunks_of, blocks_of, *refs):
    listed, spread, acc, summed, result = refs
    row, lane = rows_and_lanes()
    n_bins = cells[0] * cells[1] * cells[2]
    bins = [(i, j, k) for i in range(cells[0]) for j in range(cells[1]) for k in range(cells[2])]
    sources, counts = [], []
    for at in bins:
        moved = jnp.zeros((ROWS, LANES), jnp.float32)
        for i in range(3):
            moved = jnp.where(row == i, SPLIT_XI * (at[i] - 0.5 * (cells[i] - 1)), moved)
        counts.append(count_ref[at])
        sources.append((own_ref[at] + moved, counts[-1]))
    filled = compact(listed, 0, sources)
    n_tiles = lax.div(filled + LANES - 1, LANES)
    n_blocks = lax.div(filled + BLOCK - 1, BLOCK)
    blocks_of[0] = n_blocks
    chunks_of[0] = lax.div(filled + CHUNK - 1, CHUNK)

    def prepare(tile_id, carry):
        spread_targets(spread, pl.multiple_of(tile_id * LANES, LANES), listed[tile_id])
        return carry

    lax.fori_loop(0, n_tiles, prepare, 0)
    refs = (listed, spread, acc, summed)
    all_pairs(1, chunks_of, blocks_of, n_bins * LANES // CHUNK, n_bins // WIDE, refs)

    def finish(tile_id, carry):
        sums = jnp.transpose(summed[pl.ds(pl.multiple_of(tile_id * LANES, LANES), LANES), :])[:ROWS]
        tile = listed[tile_id]
        own = pltpu.roll(tile, ROWS - FORCE_ROW, 0)
        result[tile_id] = (2.0 * STOKES_NORM) * sums - (STOKES_NORM * SELF_C) * own
        return carry

    lax.fori_loop(0, n_tiles, finish, 0)
    before = jnp.int32(0)
    for at, count in zip(bins, counts):
        tile_id = lax.shift_right_logical(before, 7)
        back = LANES - lax.bitwise_and(before, LANES - 1)
        turn = lax.bitwise_and(back, LANES - 1)
        part = jnp.where(
            lane < back, pltpu.roll(result[tile_id], turn, 1), pltpu.roll(result[tile_id + 1], turn, 1)
        )
        out_ref[at] = part
        before = before + count


def outer_kernel(cells, *refs):
    pieces, (inner_ref, out_ref), refs = refs[:6], refs[6:8], refs[8:]
    ext, count_v, count_s, sem, chunks_of, blocks_of = refs[:6]
    listed, spread, acc, summed = refs[6:]
    own, other, x_lo, x_hi, y_lo, y_hi = pieces
    size_x, size_y, size_z = cells
    n_z = 2 * size_z
    n_bins = size_x * size_y * size_z
    row, lane = rows_and_lanes()

    held = jnp.zeros((ROWS, LANES), jnp.float32)
    for ix in range(size_x + 2):
        for iy in range(size_y + 2):
            for iz in range(n_z):
                if iy == 0:
                    tile = y_lo[ix, 0, iz]
                elif iy == size_y + 1:
                    tile = y_hi[ix, 0, iz]
                elif ix == 0:
                    tile = x_lo[0, iy - 1, iz]
                elif ix == size_x + 1:
                    tile = x_hi[0, iy - 1, iz]
                elif iz < size_z:
                    tile = own[ix - 1, iy - 1, iz]
                else:
                    tile = other[ix - 1, iy - 1, iz - size_z]
                cell = (ix * (size_y + 2) + iy) * n_z + iz
                ext[cell] = tile
                held = jnp.where(lane == cell, tile, held)
    count_v[...] = held.astype(jnp.int32)
    copy = pltpu.make_async_copy(count_v, count_s, sem)
    copy.start()
    copy.wait()

    max_tiles = listed.shape[0] // n_bins
    steps = [
        (a, b, c) for a in (0, -1, 1) for b in (0, -1, 1) for c in (0, -1, 1) if 1 in (a, b, c)
    ]

    def prepare(flat_id, carry):
        at = (flat_id // (size_y * size_z), flat_id // size_z % size_y, flat_id % size_z)
        out = [2 * i - 1 for i in at]
        moves = [
            jnp.where(row == i, (SPLIT_XI * out[i].astype(jnp.float32)), 0.0) for i in range(3)
        ]
        sources = []
        for step in steps:
            moved = sum(s * m for s, m in zip(step, moves) if s != 0)
            x, y, z = (i + s * o for i, s, o in zip(at, step, out))
            cell = ((x + 1) * (size_y + 2) + y + 1) * n_z + lax.rem(z + n_z, n_z)
            sources.append((ext[cell] + moved, count_s[COUNT_ROW, cell]))
        filled = compact(listed, flat_id * max_tiles, sources)
        n_blocks = lax.div(filled + BLOCK - 1, BLOCK)
        own_cell = ((at[0] + 1) * (size_y + 2) + at[1] + 1) * n_z + at[2]
        blocks_of[flat_id] = n_blocks
        chunks_of[flat_id] = lax.div(count_s[COUNT_ROW, own_cell] + CHUNK - 1, CHUNK)

        spread_targets(spread, pl.multiple_of(flat_id * LANES, LANES), ext[own_cell])
        return carry

    lax.fori_loop(0, n_bins, prepare, 0)
    refs = (listed, spread, acc, summed)
    all_pairs(n_bins, chunks_of, blocks_of, LANES // CHUNK, max_tiles // WIDE, refs)

    slot = lax.broadcasted_iota(jnp.int32, (1, LANES), 1)
    for ix in range(size_x):
        for iy in range(size_y):
            for iz in range(size_z):
                flat_id = (ix * size_y + iy) * size_z + iz
                sums = jnp.transpose(summed[flat_id * LANES : (flat_id + 1) * LANES, :])[:ROWS]
                total = (2.0 * STOKES_NORM) * sums + inner_ref[ix, iy, iz]
                count = count_s[COUNT_ROW, ((ix + 1) * (size_y + 2) + iy + 1) * n_z + iz]
                for i in range(3):
                    out_ref[i, ix, iy, iz : iz + 1, :] = jnp.where(
                        slot < count, total[i : i + 1], 0.0
                    )


def shifted(array, axis, dim):
    size, length = lax.axis_size(axis), array.shape[dim]
    up = [(i, (i + 1) % size) for i in range(size)]
    down = [(j, i) for i, j in up]
    before = lax.ppermute(lax.slice_in_dim(array, length - 1, length, axis=dim), axis, up)
    after = lax.ppermute(lax.slice_in_dim(array, 0, 1, axis=dim), axis, down)
    return before, after


def pair_scratch(n_targets, n_tiles):
    return [
        pltpu.VMEM((n_tiles, ROWS, LANES), jnp.float32),
        pltpu.VMEM((3, n_targets, LANES), jnp.float32),
        pltpu.VMEM((3, CHUNK, LANES), jnp.float32),
        pltpu.VMEM((n_targets, LANES), jnp.float32),
    ]


def on_device(offsets, forces, counts):
    cells = offsets.shape[1:4]
    slots = offsets.shape[4]
    n_bins = cells[0] * cells[1] * cells[2]
    n_cells = (cells[0] + 2) * (cells[1] + 2) * 2 * cells[2]
    whole = pl.BlockSpec(memory_space=pltpu.VMEM)
    scalars = pl.BlockSpec(memory_space=pltpu.SMEM)
    tiles = jax.ShapeDtypeStruct(cells + (ROWS, slots), jnp.float32)
    own = pl.pallas_call(
        functools.partial(pack_kernel, cells),
        out_shape=tiles,
        in_specs=[scalars, whole, whole],
        out_specs=whole,
        name="pack",
    )(counts, offsets, forces)

    size = lax.axis_size("ha")
    other = lax.ppermute(own, "ha", [(i, (i + 1) % size) for i in range(size)])
    params = pltpu.CompilerParams(vmem_limit_bytes=24 << 20)
    inner = pl.pallas_call(
        functools.partial(inner_kernel, cells),
        out_shape=tiles,
        in_specs=[scalars, whole],
        out_specs=whole,
        scratch_shapes=[pltpu.SMEM((1,), jnp.int32), pltpu.SMEM((1,), jnp.int32)]
        + pair_scratch(n_bins * LANES, n_bins + WIDE)
        + [pltpu.VMEM((n_bins + 2, ROWS, LANES), jnp.float32)],
        compiler_params=params,
        cost_estimate=pl.CostEstimate(flops=1 << 30, bytes_accessed=1 << 16, transcendentals=1 << 22),
        name="inner",
    )(counts, own)
    other, inner = lax.optimization_barrier((other, inner))
    column = jnp.concatenate([own, other], axis=2)
    x_lo, x_hi = shifted(column, "gx", 0)
    wide = jnp.concatenate([x_lo, column, x_hi], axis=0)
    y_lo, y_hi = shifted(wide, "gy", 1)

    max_tiles = 20 + WIDE
    return pl.pallas_call(
        functools.partial(outer_kernel, cells),
        out_shape=jax.ShapeDtypeStruct((3,) + cells + (slots,), jnp.float32),
        in_specs=[whole] * 7,
        out_specs=whole,
        scratch_shapes=[
            pltpu.VMEM((n_cells, ROWS, LANES), jnp.float32),
            pltpu.VMEM((ROWS, LANES), jnp.int32),
            pltpu.SMEM((ROWS, LANES), jnp.int32),
            pltpu.SemaphoreType.DMA,
            pltpu.SMEM((n_bins,), jnp.int32),
            pltpu.SMEM((n_bins,), jnp.int32),
        ]
        + pair_scratch(n_bins * LANES, n_bins * max_tiles),
        compiler_params=params,
        name="outer",
    )(own, other, x_lo, x_hi, y_lo, y_hi, inner)


def solution(mesh):
    in_specs = (
        P(None, "gx", "gy", "ha", None),
        P(None, "gx", "gy", "ha", None),
        P("gx", "gy", "ha"),
    )
    out_specs = P(None, "gx", "gy", "ha", None)
    return jax.shard_map(on_device, mesh=mesh, in_specs=in_specs, out_specs=out_specs, check_vma=False)
```

profile of v0, /device:TPU:0, one launch (start us, length us, event | category | flops | bytes accessed | tf_op | source)
XLA Modules:
  0.0 38.0 jit_solution(2665333539863312318)
XLA Ops:
  0.0 0.0 copy-start.2
  0.0 1.5 %pack.1.own_ref.refs_0_ = f32[2,2,2,8,128]{4,3,2,1,0:T(8,128)} custom-call(s32[2,2,2]{2,1,0:T(2,128)} %count_ref.3, f32[3,2,2,2,128]{4,3,2,1,0:T(2,128)} %offset_ref.1, f32[3,2,2,2,128]{4,3,2,1,0:T(2,128)} %force_ref.1), custom_call_target="tpu_custom_call" | custom-call | tf_op jit(solution)/shard_map/pack/pallas_call | solution.py:298
  1.5 3.0 %collective-permute-start = (f32[2,2,2,8,128]{4,3,2,1,0:T(8,128)}, f32[2,2,2,8,128]{4,3,2,1,0:T(8,128)S(1)}, u32[]{:S(2)}, u32[]{:S(2)}) collective-permute-start(f32[2,2,2,8,128]{4,3,2,1,0:T(8,128)} %pack.1.own_ref.refs_0_), channel_id=1, source_target_pairs={{0,1},{1,0},{2,3},{3,2},{4,5},{5,4},{6,7},{7,6},{8,9},{9,8},{10,11... | collective-permute-start | bytes 98312 | tf_op jit(solution)/shard_map/ppermute | solution.py:307
  4.4 0.0 copy-done.2
  4.4 0.0 copy-start
  4.4 0.8 %copy-done = f32[2,2,2,8,128]{4,3,2,1,0:T(8,128)S(1)} copy-done((f32[2,2,2,8,128]{4,3,2,1,0:T(8,128)S(1)}, f32[2,2,2,8,128]{4,3,2,1,0:T(8,128)}, u32[]{:S(2)}) %copy-start) | copy-done | bytes 32792
  5.2 10.0 %inner.1.refs_6_ = f32[2,2,2,8,128]{4,3,2,1,0:T(8,128)S(1)} custom-call(s32[2,2,2]{2,1,0:T(2,128)S(1)} %copy-done.2, f32[2,2,2,8,128]{4,3,2,1,0:T(8,128)S(1)} %copy-done), custom_call_target="tpu_custom_call" | custom-call | flops 1073741824 | bytes 65536 | tf_op jit(solution)/shard_map/inner/pallas_call | solution.py:309
  15.2 0.0 collective-permute-done.refs_1_
  15.2 0.1 collective-permute-start.2
  15.3 2.0 %collective-permute-start.1 = (f32[1,2,4,8,128]{4,3,2,1,0:T(8,128)S(1)}, f32[1,2,4,8,128]{4,3,2,1,0:T(8,128)S(1)}, u32[]{:S(2)}, u32[]{:S(2)}) collective-permute-start(f32[1,2,4,8,128]{4,3,2,1,0:T(8,128)S(1)} %get-tuple-element.12), channel_id=1, source_target_pairs={{0,8},{8,16},{16,24},{24,0},{1,9},{9,17},{17,25},{25,1},{2,10},{10... | collective-permute-start | bytes 98312 | tf_op jit(solution)/shard_map/ppermute | solution.py:276
  17.3 1.9 %collective-permute-done.2.refs_3_ = f32[1,2,4,8,128]{4,3,2,1,0:T(8,128)S(1)} collective-permute-done((f32[1,2,4,8,128]{4,3,2,1,0:T(8,128)S(1)}, f32[1,2,4,8,128]{4,3,2,1,0:T(8,128)S(1)}, u32[]{:S(2)}, u32[]{:S(2)}) %collective-permute-start.2) | collective-permute-done | bytes 32800 | tf_op jit(solution)/shard_map/ppermute | solution.py:277
  19.2 1.9 %collective-permute-done.1.refs_2_ = f32[1,2,4,8,128]{4,3,2,1,0:T(8,128)S(1)} collective-permute-done((f32[1,2,4,8,128]{4,3,2,1,0:T(8,128)S(1)}, f32[1,2,4,8,128]{4,3,2,1,0:T(8,128)S(1)}, u32[]{:S(2)}, u32[]{:S(2)}) %collective-permute-start.1) | collective-permute-done | bytes 32800 | tf_op jit(solution)/shard_map/ppermute | solution.py:276
  21.1 0.0 copy-start.1
  21.1 0.1 collective-permute-start.4
  21.2 0.5 %collective-permute-start.3 = (f32[4,1,4,8,128]{4,3,2,1,0:T(8,128)S(1)}, f32[4,1,4,8,128]{4,3,2,1,0:T(8,128)S(1)}, u32[]{:S(2)}, u32[]{:S(2)}) collective-permute-start(f32[4,1,4,8,128]{4,3,2,1,0:T(8,128)S(1)} %get-tuple-element.10), channel_id=1, source_target_pairs={{0,2},{2,4},{4,6},{6,0},{1,3},{3,5},{5,7},{7,1},{8,10},{10,12},{12... | collective-permute-start | bytes 196616 | tf_op jit(solution)/shard_map/ppermute | solution.py:276
  21.7 1.8 %collective-permute-done.4.refs_5_ = f32[4,1,4,8,128]{4,3,2,1,0:T(8,128)S(1)} collective-permute-done((f32[4,1,4,8,128]{4,3,2,1,0:T(8,128)S(1)}, f32[4,1,4,8,128]{4,3,2,1,0:T(8,128)S(1)}, u32[]{:S(2)}, u32[]{:S(2)}) %collective-permute-start.4) | collective-permute-done | bytes 65568 | tf_op jit(solution)/shard_map/ppermute | solution.py:277
  23.5 1.4 %collective-permute-done.3.refs_4_ = f32[4,1,4,8,128]{4,3,2,1,0:T(8,128)S(1)} collective-permute-done((f32[4,1,4,8,128]{4,3,2,1,0:T(8,128)S(1)}, f32[4,1,4,8,128]{4,3,2,1,0:T(8,128)S(1)}, u32[]{:S(2)}, u32[]{:S(2)}) %collective-permute-start.3) | collective-permute-done | bytes 65568 | tf_op jit(solution)/shard_map/ppermute | solution.py:276
  24.9 0.0 copy-done.1
  24.9 13.1 %outer.1 = f32[3,2,2,2,128]{4,3,2,1,0:T(2,128)} custom-call(f32[2,2,2,8,128]{4,3,2,1,0:T(8,128)S(1)} %copy-done.1, f32[2,2,2,8,128]{4,3,2,1,0:T(8,128)S(1)} %collective-permute-done.refs_1_, f32[1,2,4,8,128]{4,3,2,1,0:T(8,128)S(1)} %collective-permute-done.1.refs_2_, f32[1,2,4,8,128]{4,3,2,1,0:T(8,128)S(1)} %collective-permute-done.2.refs_3_, ...), custom_call_target="tpu_custom_call" | custom-call | tf_op jit(solution)/shard_map/outer/pallas_call | solution.py:328
  (3 shorter events, 0.0 us)
Async XLA Ops:
  0.0 4.4 %copy-start.2 = (s32[2,2,2]{2,1,0:T(2,128)S(1)}, s32[2,2,2]{2,1,0:T(2,128)}, u32[]{:S(2)}) copy-start(s32[2,2,2]{2,1,0:T(2,128)} %count_ref.3) | copy-start | bytes 100
  1.5 13.8 %collective-permute-start = (f32[2,2,2,8,128]{4,3,2,1,0:T(8,128)}, f32[2,2,2,8,128]{4,3,2,1,0:T(8,128)S(1)}, u32[]{:S(2)}, u32[]{:S(2)}) collective-permute-start(f32[2,2,2,8,128]{4,3,2,1,0:T(8,128)} %pack.1.own_ref.refs_0_), channel_id=1, source_target_pairs={{0,1},{1,0},{2,3},{3,2},{4,5},{5,4},{6,7},{7,6},{8,9},{9,8},{10,11... | collective-permute-start | bytes 98312 | tf_op jit(solution)/shard_map/ppermute | solution.py:307
  4.4 0.8 %copy-start = (f32[2,2,2,8,128]{4,3,2,1,0:T(8,128)S(1)}, f32[2,2,2,8,128]{4,3,2,1,0:T(8,128)}, u32[]{:S(2)}) copy-start(f32[2,2,2,8,128]{4,3,2,1,0:T(8,128)} %pack.1.own_ref.refs_0_) | copy-start | bytes 98308
  15.2 4.0 %collective-permute-start.2 = (f32[1,2,4,8,128]{4,3,2,1,0:T(8,128)S(1)}, f32[1,2,4,8,128]{4,3,2,1,0:T(8,128)S(1)}, u32[]{:S(2)}, u32[]{:S(2)}) collective-permute-start(f32[1,2,4,8,128]{4,3,2,1,0:T(8,128)S(1)} %get-tuple-element.11), channel_id=1, source_target_pairs={{8,0},{16,8},{24,16},{0,24},{9,1},{17,9},{25,17},{1,25},{10,2},{18... | collective-permute-start | bytes 98312 | tf_op jit(solution)/shard_map/ppermute | solution.py:277
  15.3 5.8 %collective-permute-start.1 = (f32[1,2,4,8,128]{4,3,2,1,0:T(8,128)S(1)}, f32[1,2,4,8,128]{4,3,2,1,0:T(8,128)S(1)}, u32[]{:S(2)}, u32[]{:S(2)}) collective-permute-start(f32[1,2,4,8,128]{4,3,2,1,0:T(8,128)S(1)} %get-tuple-element.12), channel_id=1, source_target_pairs={{0,8},{8,16},{16,24},{24,0},{1,9},{9,17},{17,25},{25,1},{2,10},{10... | collective-permute-start | bytes 98312 | tf_op jit(solution)/shard_map/ppermute | solution.py:276
  21.1 3.8 %copy-start.1 = (f32[2,2,2,8,128]{4,3,2,1,0:T(8,128)S(1)}, f32[2,2,2,8,128]{4,3,2,1,0:T(8,128)}, u32[]{:S(2)}) copy-start(f32[2,2,2,8,128]{4,3,2,1,0:T(8,128)} %pack.1.own_ref.refs_0_) | copy-start | bytes 98308
  21.1 2.4 %collective-permute-start.4 = (f32[4,1,4,8,128]{4,3,2,1,0:T(8,128)S(1)}, f32[4,1,4,8,128]{4,3,2,1,0:T(8,128)S(1)}, u32[]{:S(2)}, u32[]{:S(2)}) collective-permute-start(f32[4,1,4,8,128]{4,3,2,1,0:T(8,128)S(1)} %get-tuple-element.9), channel_id=1, source_target_pairs={{2,0},{4,2},{6,4},{0,6},{3,1},{5,3},{7,5},{1,7},{10,8},{12,10},{14... | collective-permute-start | bytes 196616 | tf_op jit(solution)/shard_map/ppermute | solution.py:277
  21.2 3.7 %collective-permute-start.3 = (f32[4,1,4,8,128]{4,3,2,1,0:T(8,128)S(1)}, f32[4,1,4,8,128]{4,3,2,1,0:T(8,128)S(1)}, u32[]{:S(2)}, u32[]{:S(2)}) collective-permute-start(f32[4,1,4,8,128]{4,3,2,1,0:T(8,128)S(1)} %get-tuple-element.10), channel_id=1, source_target_pairs={{0,2},{2,4},{4,6},{6,0},{1,3},{3,5},{5,7},{7,1},{8,10},{10,12},{12... | collective-permute-start | bytes 196616 | tf_op jit(solution)/shard_map/ppermute | solution.py:276
where the time goes:
time: 37.5 us; the launch traced here: 38 us
  Pallas kernels  24.6 us (66%)
  waiting for transfers between devices  7 us (19%)
  starting transfers between devices  5.59 us (15%)
  local copies, waits for them, and re-layouts  0.81 us (2%)
    pallas_call x1, Pallas kernels, on_device(): pl.pallas_call(functools.partial(outer_kernel, cells), out_shape=jax.Shap...  13.1 us
    pallas_call x1, Pallas kernels, on_device(): pl.pallas_call(functools.partial(inner_kernel, cells), out_shape=tiles, i...  9.99 us
    ppermute x2, waiting for transfers between devices, shifted(): after = lax.ppermute(lax.slice_in_dim(array, 0, 1, axis=dim), axis, down)  3.69 us
    ppermute x2, waiting for transfers between devices, shifted(): lax.ppermute(lax.slice_in_dim(array, length - 1, length, axis=dim), axis,...  3.31 us
    ppermute x1, starting transfers between devices, on_device(): other = lax.ppermute(own, 'ha', [(i, (i + 1) % size) for i in range(size)])  2.97 us
    ppermute x2, starting transfers between devices, shifted(): lax.ppermute(lax.slice_in_dim(array, length - 1, length, axis=dim), axis,...  2.51 us
    pallas_call x1, Pallas kernels, on_device(): pl.pallas_call(functools.partial(pack_kernel, cells), out_shape=tiles, in...  1.46 us
    unnamed x6, local copies, waits for them, and re-layouts  0.8 us
  transfers between devices with their start and end apart: 5, of which 4 were waited for; matrix products, arithmetic and copies ran while one was open for 0% of the time, Pallas kernels for 26%

commit v1 on v0

--- a/solution.py
+++ b/solution.py
@@ -22,10 +22,9 @@
 
 LANES = 128
 ROWS = 8
-CHUNK = 64
+CHUNK = 32
 WIDE = 2
 BLOCK = WIDE * LANES
-GROUP = 16
 COUNT_ROW = 3
 FORCE_ROW = 4
 
@@ -78,75 +77,89 @@
         spread[i, pl.ds(first, LANES), :] = jnp.broadcast_to(columns[:, i : i + 1], (LANES, LANES))
 
 
-def pair_terms(target, source, force):
+def coefficients(target, source):
     delta = [t - s for t, s in zip(target, source)]
     u = (delta[0] * delta[0] + SOFT_U) + delta[1] * delta[1] + delta[2] * delta[2]
     inv = lax.rsqrt(u)
     tail = (1.0 - lax.erf(u * inv)) * inv
     gauss = jnp.exp2(LOG2_G - u * LOG2_E)
     rest = gauss * (u - 1.5)
-    coef_c = tail + rest
-    coef_d = ((tail - rest) - gauss) * (inv * inv)
+    return tail + rest, ((tail - rest) - gauss) * (inv * inv)
+
+
+def velocity_terms(target, source, force, coef_c, coef_d):
+    delta = [t - s for t, s in zip(target, source)]
     along = coef_d * (delta[0] * force[0] + delta[1] * force[1] + delta[2] * force[2])
     return [coef_c * f + along * d for f, d in zip(force, delta)]
 
 
 def all_pairs(n_groups, chunks_of, blocks_of, max_chunks, max_blocks, refs):
-    listed, spread, acc, summed = refs
-
-    def process(group, chunk, block):
-        sources = []
-        for b in range(WIDE):
-            tile_id = (group * max_blocks + block) * WIDE + b
-            rows = [listed[tile_id, i : i + 1, :] for i in (0, 1, 2, 4, 5, 6)]
-            sources.append((rows[:3], rows[3:]))
-        first = (group * max_chunks + chunk) * CHUNK
-        for r in range(0, CHUNK, GROUP):
-            at = pl.ds(pl.multiple_of(first + r, GROUP), GROUP)
-            target = [spread[i, at, :] for i in range(3)]
-            sums = None
-            for source, force in sources:
-                terms = pair_terms(target, source, force)
-                sums = terms if sums is None else [s + t for s, t in zip(sums, terms)]
-            for i in range(3):
-                acc[i, r : r + GROUP, :] = acc[i, r : r + GROUP, :] + sums[i]
-
-    def reduce(group, chunk):
-        _, lane = rows_and_lanes((CHUNK, LANES))
-        merged = jnp.zeros((CHUNK, LANES), jnp.float32)
-        for i in range(3):
-            merged = jnp.where(lane == i, jnp.sum(acc[i], axis=1, keepdims=True), merged)
-            acc[i] = jnp.zeros((CHUNK, LANES), jnp.float32)
-        at = pl.multiple_of((group * max_chunks + chunk) * CHUNK, CHUNK)
-        summed[pl.ds(at, CHUNK), :] = merged
+    listed, spread, coefs, acc = refs
+    components = range(3)
+
+    def targets(first):
+        at = pl.ds(pl.multiple_of(first, CHUNK), CHUNK)
+        return [spread[i, at, :] for i in components]
+
+    def rows(tile_id, at):
+        return [[listed[tile_id + b, i : i + 1, :] for i in at] for b in range(WIDE)]
 
     total = jnp.int32(0)
     for group in range(n_groups):
         total = total + chunks_of[group] * blocks_of[group]
     acc[...] = jnp.zeros_like(acc)
+    coefs[...] = jnp.zeros_like(coefs)
 
     def one_item(item, state):
-        group, chunk, block = state
+        group, chunk, block, old_first, old_tile = state
+        new_first = (group * max_chunks + chunk) * CHUNK
+        new_tile = (group * max_blocks + block) * WIDE
+        old_at = pl.ds(pl.multiple_of(old_first, CHUNK), CHUNK)
+        old_coefs = [(coefs[b, 0], coefs[b, 1]) for b in range(WIDE)]
+        sums = [acc[i, old_at, :] for i in components]
+        old_target, old_source = targets(old_first), rows(old_tile, (0, 1, 2))
+        old_force = rows(old_tile, (4, 5, 6))
+        new_target, new_source = targets(new_first), rows(new_tile, (0, 1, 2))
+
+        new_coefs = [coefficients(new_target, source) for source in new_source]
+        for pair in zip(old_source, old_force, old_coefs):
+            terms = velocity_terms(old_target, pair[0], pair[1], *pair[2])
+            sums = [s + t for s, t in zip(sums, terms)]
+
+        for i in components:
+            acc[i, old_at, :] = sums[i]
+        for b in range(WIDE):
+            coefs[b, 0], coefs[b, 1] = new_coefs[b]
+
         end_block = block + 1 == blocks_of[group]
         next_block = jnp.where(end_block, 0, block + 1)
         next_chunk = jnp.where(end_block, chunk + 1, chunk)
         end_chunk = next_chunk == chunks_of[group]
         next_chunk = jnp.where(end_chunk, 0, next_chunk)
         next_group = jnp.where(end_chunk, jnp.minimum(group + 1, n_groups - 1), group)
-        process(group, chunk, block)
-
-        @pl.when(end_block)
-        def _():
-            reduce(group, chunk)
-
-        return next_group, next_chunk, next_block
-
-    zero = jnp.int32(0)
-    lax.fori_loop(0, total, one_item, (zero, zero, zero))
+        return next_group, next_chunk, next_block, new_first, new_tile
+
+    lax.fori_loop(0, total + 1, one_item, (jnp.int32(0),) * 5)
+
+
+def lane_sums(acc, first):
+    row, _ = rows_and_lanes()
+    one = jnp.ones((ROWS, LANES), jnp.float32)
+    merged = jnp.zeros((ROWS, LANES), jnp.float32)
+    for i in range(3):
+        sums = lax.dot_general(
+            one,
+            acc[i, pl.ds(first, LANES), :],
+            (((1,), (1,)), ((), ())),
+            precision=lax.Precision.HIGHEST,
+            preferred_element_type=jnp.float32,
+        )
+        merged = jnp.where(row == i, sums, merged)
+    return merged
 
 
 def inner_kernel(cells, count_ref, own_ref, out_ref, chunks_of, blocks_of, *refs):
-    listed, spread, acc, summed, result = refs
+    listed, spread, coefs, acc, result = refs
     row, lane = rows_and_lanes()
     n_bins = cells[0] * cells[1] * cells[2]
     bins = [(i, j, k) for i in range(cells[0]) for j in range(cells[1]) for k in range(cells[2])]
@@ -168,11 +181,11 @@
         return carry
 
     lax.fori_loop(0, n_tiles, prepare, 0)
-    refs = (listed, spread, acc, summed)
+    refs = (listed, spread, coefs, acc)
     all_pairs(1, chunks_of, blocks_of, n_bins * LANES // CHUNK, n_bins // WIDE, refs)
 
     def finish(tile_id, carry):
-        sums = jnp.transpose(summed[pl.ds(pl.multiple_of(tile_id * LANES, LANES), LANES), :])[:ROWS]
+        sums = lane_sums(acc, pl.multiple_of(tile_id * LANES, LANES))
         tile = listed[tile_id]
         own = pltpu.roll(tile, ROWS - FORCE_ROW, 0)
         result[tile_id] = (2.0 * STOKES_NORM) * sums - (STOKES_NORM * SELF_C) * own
@@ -194,7 +207,7 @@
 def outer_kernel(cells, *refs):
     pieces, (inner_ref, out_ref), refs = refs[:6], refs[6:8], refs[8:]
     ext, count_v, count_s, sem, chunks_of, blocks_of = refs[:6]
-    listed, spread, acc, summed = refs[6:]
+    listed, spread, coefs, acc = refs[6:]
     own, other, x_lo, x_hi, y_lo, y_hi = pieces
     size_x, size_y, size_z = cells
     n_z = 2 * size_z
@@ -252,7 +265,7 @@
         return carry
 
     lax.fori_loop(0, n_bins, prepare, 0)
-    refs = (listed, spread, acc, summed)
+    refs = (listed, spread, coefs, acc)
     all_pairs(n_bins, chunks_of, blocks_of, LANES // CHUNK, max_tiles // WIDE, refs)
 
     slot = lax.broadcasted_iota(jnp.int32, (1, LANES), 1)
@@ -260,7 +273,7 @@
         for iy in range(size_y):
             for iz in range(size_z):
                 flat_id = (ix * size_y + iy) * size_z + iz
-                sums = jnp.transpose(summed[flat_id * LANES : (flat_id + 1) * LANES, :])[:ROWS]
+                sums = lane_sums(acc, flat_id * LANES)
                 total = (2.0 * STOKES_NORM) * sums + inner_ref[ix, iy, iz]
                 count = count_s[COUNT_ROW, ((ix + 1) * (size_y + 2) + iy + 1) * n_z + iz]
                 for i in range(3):
@@ -282,8 +295,8 @@
     return [
         pltpu.VMEM((n_tiles, ROWS, LANES), jnp.float32),
         pltpu.VMEM((3, n_targets, LANES), jnp.float32),
-        pltpu.VMEM((3, CHUNK, LANES), jnp.float32),
-        pltpu.VMEM((n_targets, LANES), jnp.float32),
+        pltpu.VMEM((WIDE, 2, CHUNK, LANES), jnp.float32),
+        pltpu.VMEM((3, n_targets, LANES), jnp.float32),
     ]
 
 

time: 37.5 us -> 40.7 us (1.085); the launches traced: 38 us -> 40.3 us
  Pallas kernels: 24.6 us -> 26.8 us
    pallas_call x1, Pallas kernels: 9.99 us -> 11.6 us  [on_device(): pl.pallas_call(functools.partial(inner_kernel, cells), out_shape=tiles, i...]
    pallas_call x1, Pallas kernels: 13.1 us -> 13.7 us  [on_device(): pl.pallas_call(functools.partial(outer_kernel, cells), out_shape=jax.Shap...]
  transfers between devices with their start and end apart: 5 -> 5, of which waited for: 4 -> 4; matrix products, arithmetic and copies ran while one was open for 0% -> 0% of each run, Pallas kernels for 26% -> 29%
where the time goes in v1:
time: 40.7 us; the launch traced here: 40.3 us
  Pallas kernels  26.8 us (66%)
  waiting for transfers between devices  7 us (17%)
  starting transfers between devices  5.59 us (14%)
  local copies, waits for them, and re-layouts  0.81 us (2%)
    pallas_call x1, Pallas kernels, on_device(): pl.pallas_call(functools.partial(outer_kernel, cells), out_shape=jax.Shap...  13.7 us
    pallas_call x1, Pallas kernels, on_device(): pl.pallas_call(functools.partial(inner_kernel, cells), out_shape=tiles, i...  11.6 us
    ppermute x2, waiting for transfers between devices, shifted(): after = lax.ppermute(lax.slice_in_dim(array, 0, 1, axis=dim), axis, down)  3.69 us
    ppermute x2, waiting for transfers between devices, shifted(): lax.ppermute(lax.slice_in_dim(array, length - 1, length, axis=dim), axis,...  3.31 us
    ppermute x1, starting transfers between devices, on_device(): other = lax.ppermute(own, 'ha', [(i, (i + 1) % size) for i in range(size)])  2.97 us
    ppermute x2, starting transfers between devices, shifted(): lax.ppermute(lax.slice_in_dim(array, length - 1, length, axis=dim), axis,...  2.51 us
    pallas_call x1, Pallas kernels, on_device(): pl.pallas_call(functools.partial(pack_kernel, cells), out_shape=tiles, in...  1.46 us
  transfers between devices with their start and end apart: 5, of which 4 were waited for; matrix products, arithmetic and copies ran while one was open for 0% of the time, Pallas kernels for 29%

profile of v1, /device:TPU:0, one launch (start us, length us, event | category | flops | bytes accessed | tf_op | source)
XLA Modules:
  0.0 40.3 jit_solution(13210450753780633798)
XLA Ops:
  0.0 0.0 copy-start.2
  0.0 1.5 %pack.1.own_ref.refs_0_ = f32[2,2,2,8,128]{4,3,2,1,0:T(8,128)} custom-call(s32[2,2,2]{2,1,0:T(2,128)} %count_ref.3, f32[3,2,2,2,128]{4,3,2,1,0:T(2,128)} %offset_ref.1, f32[3,2,2,2,128]{4,3,2,1,0:T(2,128)} %force_ref.1), custom_call_target="tpu_custom_call" | custom-call | tf_op jit(solution)/shard_map/pack/pallas_call | solution.py:311
  1.5 3.0 %collective-permute-start = (f32[2,2,2,8,128]{4,3,2,1,0:T(8,128)}, f32[2,2,2,8,128]{4,3,2,1,0:T(8,128)S(1)}, u32[]{:S(2)}, u32[]{:S(2)}) collective-permute-start(f32[2,2,2,8,128]{4,3,2,1,0:T(8,128)} %pack.1.own_ref.refs_0_), channel_id=1, source_target_pairs={{0,1},{1,0},{2,3},{3,2},{4,5},{5,4},{6,7},{7,6},{8,9},{9,8},{10,11... | collective-permute-start | bytes 98312 | tf_op jit(solution)/shard_map/ppermute | solution.py:320
  4.4 0.0 copy-done.2
  4.4 0.0 copy-start
  4.4 0.8 %copy-done = f32[2,2,2,8,128]{4,3,2,1,0:T(8,128)S(1)} copy-done((f32[2,2,2,8,128]{4,3,2,1,0:T(8,128)S(1)}, f32[2,2,2,8,128]{4,3,2,1,0:T(8,128)}, u32[]{:S(2)}) %copy-start) | copy-done | bytes 32792
  5.2 11.6 %inner.1.refs_6_ = f32[2,2,2,8,128]{4,3,2,1,0:T(8,128)S(1)} custom-call(s32[2,2,2]{2,1,0:T(2,128)S(1)} %copy-done.2, f32[2,2,2,8,128]{4,3,2,1,0:T(8,128)S(1)} %copy-done), custom_call_target="tpu_custom_call" | custom-call | flops 1073741824 | bytes 65536 | tf_op jit(solution)/shard_map/inner/pallas_call | solution.py:322
  16.9 0.0 collective-permute-done.refs_1_
  16.9 0.1 collective-permute-start.2
  16.9 2.0 %collective-permute-start.1 = (f32[1,2,4,8,128]{4,3,2,1,0:T(8,128)S(1)}, f32[1,2,4,8,128]{4,3,2,1,0:T(8,128)S(1)}, u32[]{:S(2)}, u32[]{:S(2)}) collective-permute-start(f32[1,2,4,8,128]{4,3,2,1,0:T(8,128)S(1)} %get-tuple-element.12), channel_id=1, source_target_pairs={{0,8},{8,16},{16,24},{24,0},{1,9},{9,17},{17,25},{25,1},{2,10},{10... | collective-permute-start | bytes 98312 | tf_op jit(solution)/shard_map/ppermute | solution.py:289
  19.0 1.9 %collective-permute-done.2.refs_3_ = f32[1,2,4,8,128]{4,3,2,1,0:T(8,128)S(1)} collective-permute-done((f32[1,2,4,8,128]{4,3,2,1,0:T(8,128)S(1)}, f32[1,2,4,8,128]{4,3,2,1,0:T(8,128)S(1)}, u32[]{:S(2)}, u32[]{:S(2)}) %collective-permute-start.2) | collective-permute-done | bytes 32800 | tf_op jit(solution)/shard_map/ppermute | solution.py:290
  20.9 1.9 %collective-permute-done.1.refs_2_ = f32[1,2,4,8,128]{4,3,2,1,0:T(8,128)S(1)} collective-permute-done((f32[1,2,4,8,128]{4,3,2,1,0:T(8,128)S(1)}, f32[1,2,4,8,128]{4,3,2,1,0:T(8,128)S(1)}, u32[]{:S(2)}, u32[]{:S(2)}) %collective-permute-start.1) | collective-permute-done | bytes 32800 | tf_op jit(solution)/shard_map/ppermute | solution.py:289
  22.7 0.0 copy-start.1
  22.8 0.1 collective-permute-start.4
  22.8 0.5 %collective-permute-start.3 = (f32[4,1,4,8,128]{4,3,2,1,0:T(8,128)S(1)}, f32[4,1,4,8,128]{4,3,2,1,0:T(8,128)S(1)}, u32[]{:S(2)}, u32[]{:S(2)}) collective-permute-start(f32[4,1,4,8,128]{4,3,2,1,0:T(8,128)S(1)} %get-tuple-element.10), channel_id=1, source_target_pairs={{0,2},{2,4},{4,6},{6,0},{1,3},{3,5},{5,7},{7,1},{8,10},{10,12},{12... | collective-permute-start | bytes 196616 | tf_op jit(solution)/shard_map/ppermute | solution.py:289
  23.3 1.8 %collective-permute-done.4.refs_5_ = f32[4,1,4,8,128]{4,3,2,1,0:T(8,128)S(1)} collective-permute-done((f32[4,1,4,8,128]{4,3,2,1,0:T(8,128)S(1)}, f32[4,1,4,8,128]{4,3,2,1,0:T(8,128)S(1)}, u32[]{:S(2)}, u32[]{:S(2)}) %collective-permute-start.4) | collective-permute-done | bytes 65568 | tf_op jit(solution)/shard_map/ppermute | solution.py:290
  25.1 1.4 %collective-permute-done.3.refs_4_ = f32[4,1,4,8,128]{4,3,2,1,0:T(8,128)S(1)} collective-permute-done((f32[4,1,4,8,128]{4,3,2,1,0:T(8,128)S(1)}, f32[4,1,4,8,128]{4,3,2,1,0:T(8,128)S(1)}, u32[]{:S(2)}, u32[]{:S(2)}) %collective-permute-start.3) | collective-permute-done | bytes 65568 | tf_op jit(solution)/shard_map/ppermute | solution.py:289
  26.6 0.0 copy-done.1
  26.6 13.7 %outer.1 = f32[3,2,2,2,128]{4,3,2,1,0:T(2,128)} custom-call(f32[2,2,2,8,128]{4,3,2,1,0:T(8,128)S(1)} %copy-done.1, f32[2,2,2,8,128]{4,3,2,1,0:T(8,128)S(1)} %collective-permute-done.refs_1_, f32[1,2,4,8,128]{4,3,2,1,0:T(8,128)S(1)} %collective-permute-done.1.refs_2_, f32[1,2,4,8,128]{4,3,2,1,0:T(8,128)S(1)} %collective-permute-done.2.refs_3_, ...), custom_call_target="tpu_custom_call" | custom-call | tf_op jit(solution)/shard_map/outer/pallas_call | solution.py:341
  (3 shorter events, 0.0 us)
Async XLA Ops:
  0.0 4.4 %copy-start.2 = (s32[2,2,2]{2,1,0:T(2,128)S(1)}, s32[2,2,2]{2,1,0:T(2,128)}, u32[]{:S(2)}) copy-start(s32[2,2,2]{2,1,0:T(2,128)} %count_ref.3) | copy-start | bytes 100
  1.5 15.4 %collective-permute-start = (f32[2,2,2,8,128]{4,3,2,1,0:T(8,128)}, f32[2,2,2,8,128]{4,3,2,1,0:T(8,128)S(1)}, u32[]{:S(2)}, u32[]{:S(2)}) collective-permute-start(f32[2,2,2,8,128]{4,3,2,1,0:T(8,128)} %pack.1.own_ref.refs_0_), channel_id=1, source_target_pairs={{0,1},{1,0},{2,3},{3,2},{4,5},{5,4},{6,7},{7,6},{8,9},{9,8},{10,11... | collective-permute-start | bytes 98312 | tf_op jit(solution)/shard_map/ppermute | solution.py:320
  4.4 0.8 %copy-start = (f32[2,2,2,8,128]{4,3,2,1,0:T(8,128)S(1)}, f32[2,2,2,8,128]{4,3,2,1,0:T(8,128)}, u32[]{:S(2)}) copy-start(f32[2,2,2,8,128]{4,3,2,1,0:T(8,128)} %pack.1.own_ref.refs_0_) | copy-start | bytes 98308
  16.9 4.0 %collective-permute-start.2 = (f32[1,2,4,8,128]{4,3,2,1,0:T(8,128)S(1)}, f32[1,2,4,8,128]{4,3,2,1,0:T(8,128)S(1)}, u32[]{:S(2)}, u32[]{:S(2)}) collective-permute-start(f32[1,2,4,8,128]{4,3,2,1,0:T(8,128)S(1)} %get-tuple-element.11), channel_id=1, source_target_pairs={{8,0},{16,8},{24,16},{0,24},{9,1},{17,9},{25,17},{1,25},{10,2},{18... | collective-permute-start | bytes 98312 | tf_op jit(solution)/shard_map/ppermute | solution.py:290
  16.9 5.8 %collective-permute-start.1 = (f32[1,2,4,8,128]{4,3,2,1,0:T(8,128)S(1)}, f32[1,2,4,8,128]{4,3,2,1,0:T(8,128)S(1)}, u32[]{:S(2)}, u32[]{:S(2)}) collective-permute-start(f32[1,2,4,8,128]{4,3,2,1,0:T(8,128)S(1)} %get-tuple-element.12), channel_id=1, source_target_pairs={{0,8},{8,16},{16,24},{24,0},{1,9},{9,17},{17,25},{25,1},{2,10},{10... | collective-permute-start | bytes 98312 | tf_op jit(solution)/shard_map/ppermute | solution.py:289
  22.7 3.8 %copy-start.1 = (f32[2,2,2,8,128]{4,3,2,1,0:T(8,128)S(1)}, f32[2,2,2,8,128]{4,3,2,1,0:T(8,128)}, u32[]{:S(2)}) copy-start(f32[2,2,2,8,128]{4,3,2,1,0:T(8,128)} %pack.1.own_ref.refs_0_) | copy-start | bytes 98308
  22.8 2.4 %collective-permute-start.4 = (f32[4,1,4,8,128]{4,3,2,1,0:T(8,128)S(1)}, f32[4,1,4,8,128]{4,3,2,1,0:T(8,128)S(1)}, u32[]{:S(2)}, u32[]{:S(2)}) collective-permute-start(f32[4,1,4,8,128]{4,3,2,1,0:T(8,128)S(1)} %get-tuple-element.9), channel_id=1, source_target_pairs={{2,0},{4,2},{6,4},{0,6},{3,1},{5,3},{7,5},{1,7},{10,8},{12,10},{14... | collective-permute-start | bytes 196616 | tf_op jit(solution)/shard_map/ppermute | solution.py:290
  22.8 3.7 %collective-permute-start.3 = (f32[4,1,4,8,128]{4,3,2,1,0:T(8,128)S(1)}, f32[4,1,4,8,128]{4,3,2,1,0:T(8,128)S(1)}, u32[]{:S(2)}, u32[]{:S(2)}) collective-permute-start(f32[4,1,4,8,128]{4,3,2,1,0:T(8,128)S(1)} %get-tuple-element.10), channel_id=1, source_target_pairs={{0,2},{2,4},{4,6},{6,0},{1,3},{3,5},{5,7},{7,1},{8,10},{10,12},{12... | collective-permute-start | bytes 196616 | tf_op jit(solution)/shard_map/ppermute | solution.py:289
